TPU v7x, 32 devices: a whole 2x2x4 slice. The times are simulated.
32 devices in a mesh: comp: 8 (over y, x, core), space: 4 (over z).
Axes of the slice: x: 2, y: 2, z: 4, core: 2. Of those that a mesh axis runs over, the one named last changes fastest.
Arguments:
- concentration: float32 [16, 16, 64, 2048], P('comp', None, 'space'), may hold values from -3 to 3
- phase_labels: int32 [16, 64, 2048], P(None, 'space'), may hold values from 0 to 3
- hessian: float32 [4, 16, 16], replicated, may hold values from -1.5 to 1.5
- mobility: float32 [4, 16], replicated, may hold values from 0.2 to 2
Outputs:
- new_concentration: float32 [16, 16, 64, 2048], P('comp', None, 'space')
- potential: float32 [16, 16, 64, 2048], P('comp', None, 'space')
All inputs are finite; a program needn't handle non-finite values.
Results may differ from a plain program's by a relative error of at most 0.00017.
Values sent between devices are 32-bit elements; how exact they have to be, the bound alone decides.
A program may use at most 192 MiB of HBM per device.

v0:
```python
import jax
import jax.numpy as jnp
from jax import lax
from jax.sharding import PartitionSpec as P

SWEEPS = 2


time_step = 0.1
stiff_step = 0.02
damping = 0.5


def extended(shard, sides, width):
    for axis, dim in sides:
        devices, length = (lax.axis_size(axis), shard.shape[dim])
        up = [(i, (i + 1) % devices) for i in range(devices)]
        down = [(j, i) for i, j in up]
        last = lax.slice_in_dim(shard, length - width, length, axis=dim)
        initial = lax.slice_in_dim(shard, 0, width, axis=dim)
        before = lax.ppermute(last, axis, up)
        after = lax.ppermute(initial, axis, down)
        shard = jnp.concatenate([before, shard, after], axis=dim)
    return shard


def laplace_inner(field):
    centre = field[:, :, 1:-1, :]
    summed = field[:, :, 2:, :] + field[:, :, :-2, :]
    summed = summed + jnp.roll(centre, 1, 3) + jnp.roll(centre, -1, 3)
    summed = summed + jnp.roll(centre, 1, 1) + jnp.roll(centre, -1, 1)
    return summed - 6.0 * centre


def apply_hessian(tables, fields, phase_map):
    summed = jnp.zeros((tables.shape[1],) + fields.shape[1:], jnp.float32)
    for phase in range(tables.shape[0]):
        product = jnp.einsum(
            "ij,jzxy->izxy", tables[phase], fields, precision=lax.Precision.HIGHEST
        )
        summed = summed + jnp.where(phase_map == phase, product, 0.0)
    return summed


def on_device(concentration, phase_labels, hessian, mobility):
    local_comps = concentration.shape[0]
    comp_rank = lax.axis_index("comp")
    col_block = lax.dynamic_slice_in_dim(hessian, comp_rank * local_comps, local_comps, 2)
    potential = lax.psum_scatter(
        apply_hessian(col_block, concentration, phase_labels),
        "comp",
        scatter_dimension=0,
        tiled=True,
    )
    potential = potential + concentration * concentration * concentration
    own_mobility = lax.dynamic_slice_in_dim(mobility, comp_rank * local_comps, local_comps, 1)
    mobile = jnp.zeros(concentration.shape, jnp.float32)
    for phase in range(own_mobility.shape[0]):
        mobile = mobile + jnp.where(
            phase_labels == phase, own_mobility[phase][:, None, None, None], 0.0
        )
    padded = extended(potential, (("space", 2),), 1)
    source = concentration + time_step * mobile * laplace_inner(padded)
    bilap_coef = stiff_step * mobile
    diagonal_term = 1.0 + 42.0 * bilap_coef
    iterate = source
    for sweep in range(SWEEPS):
        widened = extended(iterate, (("space", 2),), 2)
        iterate = (
            iterate
            + damping
            * (source - iterate - bilap_coef * laplace_inner(laplace_inner(widened)))
            / diagonal_term
        )
    return (iterate, potential)


def solution(mesh):
    in_specs = (P("comp", None, "space", None), P(None, "space", None), P(), P())
    out_specs = (P("comp", None, "space", None), P("comp", None, "space", None))
    return jax.shard_map(
        on_device, mesh=mesh, in_specs=in_specs, out_specs=out_specs, check_vma=False
    )
```

profile of v0, /device:TPU:0, one launch (start us, length us, event | category | flops | bytes accessed | tf_op | source)
XLA Modules:
  0.0 635.8 jit_solution(10784087299216505486)
XLA Ops:
  7.2 0.7 copy-done
  7.9 33.7 %fusion.53 = f32[16,16,16,2048]{3,0,2,1:T(8,128)} fusion(f32[2,16,16,2048]{3,2,1,0:T(8,128)} %param.4, f32[4,16,16]{2,1,0:T(8,128)S(1)} %copy-done, s32[]{:T(128)S(6)} %select_n.30), kind=kOutput, calls=%fused_computation.85 | convolution fusion | flops 201326592 | bytes 37756932 | tf_op jit(solution)/shard_map/ij,jzxy->izxy/dot_general | solution.py:38
  41.6 30.4 %fusion.51 = f32[16,16,16,2048]{3,0,2,1:T(8,128)} fusion(f32[2,16,16,2048]{3,2,1,0:T(8,128)S(1)} %copy-done.4, f32[4,16,16]{2,1,0:T(8,128)S(1)} %copy-done, s32[]{:T(128)S(6)} %add.155, s32[]{:T(128)S(6)} %select_n.30), kind=kOutput, calls=%fused_computation.83 | convolution fusion | flops 201326592 | bytes 37756936 | tf_op jit(solution)/shard_map/ij,jzxy->izxy/dot_general | solution.py:38
  72.0 33.8 %fusion.49 = f32[16,16,16,2048]{3,0,2,1:T(8,128)} fusion(f32[2,16,16,2048]{3,2,1,0:T(8,128)} %param.4, f32[4,16,16]{2,1,0:T(8,128)S(1)} %copy-done, s32[]{:T(128)S(6)} %add.156, s32[]{:T(128)S(6)} %select_n.30), kind=kOutput, calls=%fused_computation.81 | convolution fusion | flops 201326592 | bytes 37756936 | tf_op jit(solution)/shard_map/ij,jzxy->izxy/dot_general | solution.py:38
  105.8 1.3 broadcast_compare_fusion.3
  107.1 62.9 %select_add_fusion = f32[16,16,16,2048]{3,0,2,1:T(8,128)} fusion(f32[16,16,16,2048]{3,0,2,1:T(8,128)} %fusion.49, f32[16,16,16,2048]{3,0,2,1:T(8,128)} %fusion.51, f32[16,16,16,2048]{3,0,2,1:T(8,128)} %fusion.53, pred[16,16,2048]{2,1,0:T(8,128)(4,1)S(1)} %get-tuple-element.44, pred[16,16,2048]{2,1,0:T(8,128)(4,1)S(1)} %get-tuple-element.45, ...), kind=kOutput, calls=%fused_computation | convolution fusion | flops 260046848 | bytes 140517376 | tf_op jit(solution)/shard_map/ij,jzxy->izxy/dot_general | solution.py:38
  170.1 31.9 %copy.28 = f32[16,16,16,2048]{3,2,1,0:T(8,128)} copy(f32[16,16,16,2048]{3,0,2,1:T(8,128)} %select_add_fusion) | data formatting | bytes 67108864 | tf_op jit(solution)/shard_map/add | solution.py:41
  202.0 0.6 copy-done.29
  202.8 207.4 %reduce-scatter.2.cloned.1.call-done = f32[2,16,16,2048]{3,2,1,0:T(8,128)} async-done(((f32[16,16,16,2048]{3,2,1,0:T(8,128)}), f32[2,16,16,2048]{3,2,1,0:T(8,128)}) %reduce-scatter.2.cloned.1.call-update) | async-done | bytes 4194320 | tf_op jit(solution)/shard_map/reduce_scatter | solution.py:49
  410.1 4.3 fusion.18
  414.5 4.8 fusion.75
  419.3 2.6 fusion.73
  421.9 0.4 fusion.77
  422.4 3.4 collective-permute-start
  425.7 0.8 fusion.74
  426.6 0.9 fusion.76
  427.4 5.0 collective-permute-done
  432.5 5.5 collective-permute-done.1
  438.0 14.2 %fusion.46 = f32[2,16,16,2048]{3,2,1,0:T(8,128)} fusion(f32[2,16,16,2048]{3,2,1,0:T(8,128)S(1)} %copy-done.5, f32[2,16,16,2048]{3,2,1,0:T(8,128)} %copy-done.6, f32[2,16,1,2048]{3,2,1,0:T(1,128)} %collective-permute-done.1, f32[2,16,1,2048]{3,2,1,0:T(1,128)} %collective-permute-done, f32[2,16,16,2047]{3,2,1,0:T(8,128)} %get-tuple-element.37, ...), kind=kLoop, calls=%fused_computation.75 | loop fusion | flops 24117248 | bytes 31981600 | tf_op jit(solution)/shard_map/add | solution.py:63
  452.2 2.7 fusion.72
  454.9 1.8 collective-permute-start.2
  456.7 0.3 collective-permute-start.3
  457.0 13.2 %collective-permute-done.2 = f32[2,16,2,2048]{3,2,1,0:T(2,128)S(1)} collective-permute-done((f32[2,16,2,2048]{3,2,1,0:T(2,128)S(1)}, f32[2,16,2,2048]{3,2,1,0:T(2,128)S(1)}, u32[]{:S(2)}, u32[]{:S(2)}) %collective-permute-start.2) | collective-permute-done | bytes 524320 | tf_op jit(solution)/shard_map/ppermute | solution.py:22
  470.2 8.8 %collective-permute-done.3 = f32[2,16,2,2048]{3,2,1,0:T(2,128)S(1)} collective-permute-done((f32[2,16,2,2048]{3,2,1,0:T(2,128)S(1)}, f32[2,16,2,2048]{3,2,1,0:T(2,128)S(1)}, u32[]{:S(2)}, u32[]{:S(2)}) %collective-permute-start.3) | collective-permute-done | bytes 524320 | tf_op jit(solution)/shard_map/ppermute | solution.py:21
  479.0 0.8 copy-done.24
  479.8 3.2 pad_maximum_fusion.16
  483.1 7.8 %fusion.70 = (f32[2,16,18,2047]{3,2,1,0:T(8,128)}, f32[2,16,18,2047]{3,2,1,0:T(8,128)}) fusion(f32[2,16,20,2048]{3,2,1,0:T(8,128)S(1)} %pad_maximum_fusion.16), kind=kLoop, calls=%fused_computation.115 | loop fusion | bytes 18865152 | tf_op jit(solution)/shard_map/jit(_roll_static)/slice | solution.py:30
  490.9 5.8 fusion.69
  496.7 14.5 %fusion.9 = f32[2,16,18,2048]{3,2,1,0:T(8,128)S(1)} fusion(f32[2,16,20,2048]{3,2,1,0:T(8,128)S(1)} %pad_maximum_fusion.16, f32[2,16,2,2048]{3,2,1,0:T(2,128)S(1)} %copy-done.21, f32[2,16,16,2048]{3,2,1,0:T(8,128)} %fusion.46, f32[2,16,2,2048]{3,2,1,0:T(2,128)S(1)} %copy-done.25, f32[2,16,18,2047]{3,2,1,0:T(8,128)} %get-tuple-element.27, ...), kind=kLoop, calls=%fused_computation.20 | loop fusion | flops 24772608 | bytes 32960000 | tf_op jit(solution)/shard_map/sub | solution.py:32
  511.2 5.5 fusion.67
  516.7 4.6 fusion.65
  521.3 0.8 fusion.66
  522.1 0.9 fusion.68
  523.0 15.9 %fusion.34 = f32[2,16,16,2048]{3,2,1,0:T(8,128)} fusion(f32[2,16,16,2048]{3,2,1,0:T(8,128)S(1)} %copy-done.7, f32[2,16,18,2048]{3,2,1,0:T(8,128)} %copy-done.2, f32[2,16,16,2047]{3,2,1,0:T(8,128)} %get-tuple-element.21, f32[2,16,16,1]{3,2,1,0:T(8,128)} %get-tuple-element.23, f32[2,16,16,1]{3,2,1,0:T(8,128)} %get-tuple-element.22, ...), kind=kLoop, calls=%fused_computation.61 | loop fusion | flops 28311552 | bytes 39845920 | tf_op jit(solution)/shard_map/add | solution.py:70
  538.9 2.7 fusion.71
  541.6 2.5 collective-permute-start.4
  544.1 0.2 collective-permute-start.5
  544.3 12.2 %collective-permute-done.4 = f32[2,16,2,2048]{3,2,1,0:T(2,128)S(1)} collective-permute-done((f32[2,16,2,2048]{3,2,1,0:T(2,128)S(1)}, f32[2,16,2,2048]{3,2,1,0:T(2,128)S(1)}, u32[]{:S(2)}, u32[]{:S(2)}) %collective-permute-start.4) | collective-permute-done | bytes 524320 | tf_op jit(solution)/shard_map/ppermute | solution.py:22
  556.5 12.0 %collective-permute-done.5 = f32[2,16,2,2048]{3,2,1,0:T(2,128)S(1)} collective-permute-done((f32[2,16,2,2048]{3,2,1,0:T(2,128)S(1)}, f32[2,16,2,2048]{3,2,1,0:T(2,128)S(1)}, u32[]{:S(2)}, u32[]{:S(2)}) %collective-permute-start.5) | collective-permute-done | bytes 524320 | tf_op jit(solution)/shard_map/ppermute | solution.py:21
  568.5 0.8 copy-done.26
  569.3 3.2 pad_maximum_fusion.17
  572.5 7.8 %fusion.64 = (f32[2,16,18,2047]{3,2,1,0:T(8,128)}, f32[2,16,18,2047]{3,2,1,0:T(8,128)}) fusion(f32[2,16,20,2048]{3,2,1,0:T(8,128)S(1)} %pad_maximum_fusion.17), kind=kLoop, calls=%fused_computation.109 | loop fusion | bytes 18865152 | tf_op jit(solution)/shard_map/jit(_roll_static)/slice | solution.py:30
  580.4 5.8 fusion.63
  586.1 14.3 %fusion = f32[2,16,18,2048]{3,2,1,0:T(8,128)S(1)} fusion(f32[2,16,20,2048]{3,2,1,0:T(8,128)S(1)} %pad_maximum_fusion.17, f32[2,16,2,2048]{3,2,1,0:T(2,128)S(1)} %copy-done.23, f32[2,16,16,2048]{3,2,1,0:T(8,128)} %fusion.34, f32[2,16,2,2048]{3,2,1,0:T(2,128)S(1)} %copy-done.27, f32[2,16,18,2047]{3,2,1,0:T(8,128)} %get-tuple-element.15, ...), kind=kLoop, calls=%fused_computation.2 | loop fusion | flops 24772608 | bytes 32960000 | tf_op jit(solution)/shard_map/sub | solution.py:32
  600.4 5.4 fusion.61
  605.9 4.1 fusion.59
  610.0 0.2 fusion.62
  610.2 18.2 %fusion.24 = f32[2,16,16,2048]{3,2,1,0:T(8,128)} fusion(f32[2,16,16,2048]{3,2,1,0:T(8,128)} %fusion.34, f32[2,16,18,2048]{3,2,1,0:T(8,128)} %copy-done.3, f32[2,16,16,2047]{3,2,1,0:T(8,128)} %get-tuple-element.9, f32[2,16,16,1]{3,2,1,0:T(8,128)S(1)} %get-tuple-element.11, f32[2,16,16,1]{3,2,1,0:T(8,128)S(1)} %get-tuple-element.10, ...), kind=kLoop, calls=%fused_computation.49 | loop fusion | flops 28311552 | bytes 44040224 | tf_op jit(solution)/shard_map/add | solution.py:70
  (62 shorter events, 0.3 us)
Async XLA Ops:
  7.2 0.8 copy-start
  7.2 402.9 %reduce-scatter.2.cloned.1.call-start = ((), (), s32[]{:S(2)}) async-start(), calls=%async_computation.1 | async-start | bytes 37748736 | tf_op jit(solution)/shard_map/reduce_scatter | solution.py:49
  7.9 33.7 %copy-start.4 = (f32[2,16,16,2048]{3,2,1,0:T(8,128)S(1)}, f32[2,16,16,2048]{3,2,1,0:T(8,128)}, u32[]{:S(2)}) copy-start(f32[2,16,16,2048]{3,2,1,0:T(8,128)} %param.4) | copy-start | bytes 12582916
  72.0 33.8 %copy-start.28 = (s32[16,16,2048]{2,1,0:T(8,128)S(1)}, s32[16,16,2048]{2,1,0:T(8,128)}, u32[]{:S(2)}) copy-start(s32[16,16,2048]{2,1,0:T(8,128)} %param.5) | copy-start | bytes 6291460
  107.1 62.9 %copy-start.8 = (pred[16,16,2048]{2,1,0:T(8,128)(4,1)}, pred[16,16,2048]{2,1,0:T(8,128)(4,1)S(1)}, u32[]{:S(2)}) copy-start(pred[16,16,2048]{2,1,0:T(8,128)(4,1)S(1)} %get-tuple-element.42) | copy-start | bytes 1572868
  107.1 62.9 %copy-start.11 = (pred[16,16,2048]{2,1,0:T(8,128)(4,1)}, pred[16,16,2048]{2,1,0:T(8,128)(4,1)S(1)}, u32[]{:S(2)}) copy-start(pred[16,16,2048]{2,1,0:T(8,128)(4,1)S(1)} %get-tuple-element.43) | copy-start | bytes 1572868
  107.1 62.9 %copy-start.14 = (pred[16,16,2048]{2,1,0:T(8,128)(4,1)}, pred[16,16,2048]{2,1,0:T(8,128)(4,1)S(1)}, u32[]{:S(2)}) copy-start(pred[16,16,2048]{2,1,0:T(8,128)(4,1)S(1)} %get-tuple-element.44) | copy-start | bytes 1572868
  107.1 62.9 %copy-start.17 = (pred[16,16,2048]{2,1,0:T(8,128)(4,1)}, pred[16,16,2048]{2,1,0:T(8,128)(4,1)S(1)}, u32[]{:S(2)}) copy-start(pred[16,16,2048]{2,1,0:T(8,128)(4,1)S(1)} %get-tuple-element.45) | copy-start | bytes 1572868
  202.0 0.7 copy-start.29
  414.5 12.1 %copy-start.6 = (f32[2,16,16,2048]{3,2,1,0:T(8,128)}, f32[2,16,16,2048]{3,2,1,0:T(8,128)S(1)}, u32[]{:S(2)}) copy-start(f32[2,16,16,2048]{3,2,1,0:T(8,128)S(1)} %fusion.18) | copy-start | bytes 12582916
  419.3 18.7 %copy-start.5 = (f32[2,16,16,2048]{3,2,1,0:T(8,128)S(1)}, f32[2,16,16,2048]{3,2,1,0:T(8,128)}, u32[]{:S(2)}) copy-start(f32[2,16,16,2048]{3,2,1,0:T(8,128)} %param.4) | copy-start | bytes 12582916
  422.4 10.1 %collective-permute-start = (f32[2,16,1,2048]{3,2,1,0:T(1,128)S(1)}, f32[2,16,1,2048]{3,2,1,0:T(1,128)}, u32[]{:S(2)}, u32[]{:S(2)}) collective-permute-start(f32[2,16,1,2048]{3,2,1,0:T(1,128)S(1)} %get-tuple-element.40), channel_id=1, source_target_pairs={{1,0},{2,1},{3,2},{0,3},{5,4},{6,5},{7,6},{4,7},{9,8},{10,9},{11,1... | collective-permute-start | bytes 786440 | tf_op jit(solution)/shard_map/ppermute | solution.py:22
  425.7 12.2 %collective-permute-start.1 = (f32[2,16,1,2048]{3,2,1,0:T(1,128)S(1)}, f32[2,16,1,2048]{3,2,1,0:T(1,128)}, u32[]{:S(2)}, u32[]{:S(2)}) collective-permute-start(f32[2,16,1,2048]{3,2,1,0:T(1,128)S(1)} %get-tuple-element.41), channel_id=1, source_target_pairs={{0,1},{1,2},{2,3},{3,0},{4,5},{5,6},{6,7},{7,4},{8,9},{9,10},{10,1... | collective-permute-start | bytes 786440 | tf_op jit(solution)/shard_map/ppermute | solution.py:21
  454.9 15.3 %collective-permute-start.2 = (f32[2,16,2,2048]{3,2,1,0:T(2,128)S(1)}, f32[2,16,2,2048]{3,2,1,0:T(2,128)S(1)}, u32[]{:S(2)}, u32[]{:S(2)}) collective-permute-start(f32[2,16,2,2048]{3,2,1,0:T(2,128)S(1)} %get-tuple-element.31), channel_id=1, source_target_pairs={{1,0},{2,1},{3,2},{0,3},{5,4},{6,5},{7,6},{4,7},{9,8},{10,9},{11,1... | collective-permute-start | bytes 1572872 | tf_op jit(solution)/shard_map/ppermute | solution.py:22
  456.7 22.3 %collective-permute-start.3 = (f32[2,16,2,2048]{3,2,1,0:T(2,128)S(1)}, f32[2,16,2,2048]{3,2,1,0:T(2,128)S(1)}, u32[]{:S(2)}, u32[]{:S(2)}) collective-permute-start(f32[2,16,2,2048]{3,2,1,0:T(2,128)S(1)} %get-tuple-element.30), channel_id=1, source_target_pairs={{0,1},{1,2},{2,3},{3,0},{4,5},{5,6},{6,7},{7,4},{8,9},{9,10},{10,1... | collective-permute-start | bytes 1572872 | tf_op jit(solution)/shard_map/ppermute | solution.py:21
  470.2 8.8 %copy-start.20 = (f32[2,16,2,2048]{3,2,1,0:T(2,128)}, f32[2,16,2,2048]{3,2,1,0:T(2,128)S(1)}, u32[]{:S(2)}) copy-start(f32[2,16,2,2048]{3,2,1,0:T(2,128)S(1)} %collective-permute-done.2) | copy-start | bytes 1572868
  479.0 0.8 copy-start.24
  490.9 5.8 copy-start.21
  490.9 5.8 copy-start.25
  511.2 10.9 %copy-start.2 = (f32[2,16,18,2048]{3,2,1,0:T(8,128)}, f32[2,16,18,2048]{3,2,1,0:T(8,128)S(1)}, u32[]{:S(2)}) copy-start(f32[2,16,18,2048]{3,2,1,0:T(8,128)S(1)} %fusion.9) | copy-start | bytes 14155780
  516.7 6.3 copy-start.7
  516.7 6.3 copy-start.9
  516.7 6.3 copy-start.12
  516.7 6.3 copy-start.15
  516.7 6.4 copy-start.18
  541.6 14.9 %collective-permute-start.4 = (f32[2,16,2,2048]{3,2,1,0:T(2,128)S(1)}, f32[2,16,2,2048]{3,2,1,0:T(2,128)S(1)}, u32[]{:S(2)}, u32[]{:S(2)}) collective-permute-start(f32[2,16,2,2048]{3,2,1,0:T(2,128)S(1)} %get-tuple-element.29), channel_id=1, source_target_pairs={{1,0},{2,1},{3,2},{0,3},{5,4},{6,5},{7,6},{4,7},{9,8},{10,9},{11,1... | collective-permute-start | bytes 1572872 | tf_op jit(solution)/shard_map/ppermute | solution.py:22
  544.1 24.4 %collective-permute-start.5 = (f32[2,16,2,2048]{3,2,1,0:T(2,128)S(1)}, f32[2,16,2,2048]{3,2,1,0:T(2,128)S(1)}, u32[]{:S(2)}, u32[]{:S(2)}) collective-permute-start(f32[2,16,2,2048]{3,2,1,0:T(2,128)S(1)} %get-tuple-element.28), channel_id=1, source_target_pairs={{0,1},{1,2},{2,3},{3,0},{4,5},{5,6},{6,7},{7,4},{8,9},{9,10},{10,1... | collective-permute-start | bytes 1572872 | tf_op jit(solution)/shard_map/ppermute | solution.py:21
  556.5 12.0 %copy-start.22 = (f32[2,16,2,2048]{3,2,1,0:T(2,128)}, f32[2,16,2,2048]{3,2,1,0:T(2,128)S(1)}, u32[]{:S(2)}) copy-start(f32[2,16,2,2048]{3,2,1,0:T(2,128)S(1)} %collective-permute-done.4) | copy-start | bytes 1572868
  568.5 0.8 copy-start.26
  580.4 5.8 copy-start.23
  580.4 5.8 copy-start.27
  600.4 9.7 %copy-start.3 = (f32[2,16,18,2048]{3,2,1,0:T(8,128)}, f32[2,16,18,2048]{3,2,1,0:T(8,128)S(1)}, u32[]{:S(2)}) copy-start(f32[2,16,18,2048]{3,2,1,0:T(8,128)S(1)} %fusion) | copy-start | bytes 14155780
  605.9 4.3 copy-start.10
  605.9 4.3 copy-start.13
  605.9 4.3 copy-start.16
  605.9 4.3 copy-start.19
  610.2 18.2 %copy-start.1 = (f32[4,16,16]{2,1,0:T(8,128)S(1)}, f32[4,16,16]{2,1,0:T(8,128)}, u32[]{:S(2)}) copy-start(f32[4,16,16]{2,1,0:T(8,128)} %param.6) | copy-start | bytes 12292
Sparse Core Ops, SparseCore 0:
  202.2 207.9 reduce-scatter.1
where the time goes:
time: 642 us; the launch traced here: 636 us
  waiting for transfers between devices  264 us (41%)
  matrix products  161 us (25%)
  local copies, waits for them, and re-layouts  98.7 us (15%)
  other arithmetic  89.1 us (14%)
  between operations  14.8 us (2%)
  starting transfers between devices  8.21 us (1%)
    reduce_scatter x1, waiting for transfers between devices, on_device(): lax.psum_scatter(apply_hessian(col_block, concentration, phase_labels), '...  207 us
    dot_general x4, matrix products, apply_hessian(): jnp.einsum('ij,jzxy->izxy', tables[phase], fields, precision=lax.Precisio...  161 us
    add x2, other arithmetic, on_device(): iterate + damping * (source - iterate - bilap_coef * laplace_inner(laplac...  34 us
    slice x8, local copies, waits for them, and re-layouts, laplace_inner(): summed = summed + jnp.roll(centre, 1, 3) + jnp.roll(centre, -1, 3)  33.3 us
    add x1, local copies, waits for them, and re-layouts, apply_hessian(): summed = summed + jnp.where(phase_map == phase, product, 0.0)  31.9 us
    ppermute x3, waiting for transfers between devices, extended(): after = lax.ppermute(initial, axis, down)  30.4 us
    sub x2, other arithmetic, laplace_inner(): return summed - 6.0 * centre  28.8 us
    ppermute x3, waiting for transfers between devices, extended(): before = lax.ppermute(last, axis, up)  26.3 us
  transfers between devices with their start and end apart: 7, of which 7 were waited for; matrix products, arithmetic and copies ran while one was open for 0% of the time, Pallas kernels for 0%

commit v1 on v0

--- a/solution.py
+++ b/solution.py
@@ -1,6 +1,10 @@
+import functools
+
 import jax
 import jax.numpy as jnp
 from jax import lax
+from jax.experimental import pallas as pl
+from jax.experimental.pallas import tpu as pltpu
 from jax.sharding import PartitionSpec as P
 
 SWEEPS = 2
@@ -9,6 +13,11 @@
 time_step = 0.1
 stiff_step = 0.02
 damping = 0.5
+
+MESH = pl.DeviceIdType.MESH
+DEPTH = 3
+LAG = 3
+LANES = 256
 
 
 def extended(shard, sides, width):
@@ -32,27 +41,185 @@
     return summed - 6.0 * centre
 
 
-def apply_hessian(tables, fields, phase_map):
-    summed = jnp.zeros((tables.shape[1],) + fields.shape[1:], jnp.float32)
-    for phase in range(tables.shape[0]):
-        product = jnp.einsum(
-            "ij,jzxy->izxy", tables[phase], fields, precision=lax.Precision.HIGHEST
+def potential_kernel(
+    inner, c_hbm, ph_hbm, h_ref, pot_hbm,
+    gathered, labels, part_out, part_in, pot,
+    xs, xr, os, orr, fs, fr, ys, yr, own_sem, label_sem, out_sem,
+):
+    local, nz, nx, ny = c_hbm.shape
+    phases = h_ref.shape[0]
+    me = lax.axis_index("comp")
+    core = lax.rem(me, 2)
+    spot = lax.rem(me // 2, inner)
+    row = me // (2 * inner)
+
+    def index(a, b, k):
+        return (a * inner + b) * 2 + k
+
+    sibling = index(row, spot, 1 - core)
+    across = index(1 - row, spot, core)
+    slot = spot * 2 + core
+    peers = [index(row, lax.rem(spot + d, inner), core) for d in range(1, inner)]
+    sources = [lax.rem(spot + inner - d, inner) * 2 + core for d in range(1, inner)]
+
+    def remote(src, dst, send, recv, device):
+        return pltpu.make_async_remote_copy(
+            src_ref=src, dst_ref=dst, send_sem=send, recv_sem=recv,
+            device_id={"comp": device}, device_id_type=MESH,
         )
-        summed = summed + jnp.where(phase_map == phase, product, 0.0)
-    return summed
+
+    def x_copy(d, s):
+        return remote(c_hbm.at[:, s], gathered.at[slot, :, s], xs.at[d, s], xr.at[d, s], peers[d])
+
+    def o_copy(s):
+        return remote(c_hbm.at[:, s], gathered.at[slot, :, s], os.at[s], orr.at[s], sibling)
+
+    def f_copy(d, s):
+        place = gathered.at[sources[d], :, s]
+        return remote(place, place, fs.at[d, s], fr.at[d, s], sibling)
+
+    def y_copy(s):
+        return remote(part_out.at[:, s], part_in.at[:, s], ys.at[s], yr.at[s], across)
+
+    def out_copy(s):
+        return pltpu.make_async_copy(pot.at[:, s], pot_hbm.at[:, s], out_sem.at[s])
+
+    own_copy = pltpu.make_async_copy(c_hbm, gathered.at[slot], own_sem)
+    label_copy = pltpu.make_async_copy(ph_hbm, labels, label_sem)
+    own_copy.start()
+    label_copy.start()
+
+    barrier = pltpu.get_barrier_semaphore()
+    others = peers + [sibling, across]
+    for other in others:
+        pl.semaphore_signal(barrier, inc=1, device_id={"comp": other}, device_id_type=MESH)
+    pl.semaphore_wait(barrier, len(others))
+
+    def send(s):
+        for d in range(inner - 1):
+            x_copy(d, s).start()
+        o_copy(s).start()
+
+    for s in range(min(DEPTH, nz)):
+        send(s)
+    own_copy.wait()
+    label_copy.wait()
+
+    def partials(s):
+        def block(i, carry):
+            cols = pl.ds(pl.multiple_of(i * LANES, LANES), LANES)
+            phase = labels[s, :, cols]
+            masks = [phase == p for p in range(1, phases)]
+            sums = {}
+            for j in range(2 * inner):
+                for l in range(local):
+                    value = gathered[j, l, s, :, cols]
+                    column = (row * 2 * inner + j) * local + l
+                    for side, owner in enumerate((across, me)):
+                        for o in range(local):
+                            line = owner * local + o
+                            factor = h_ref[0, line, column]
+                            for p in range(1, phases):
+                                factor = jnp.where(masks[p - 1], h_ref[p, line, column], factor)
+                            term = factor * value
+                            key = (side, o)
+                            sums[key] = sums[key] + term if key in sums else term
+            for o in range(local):
+                part_out[o, s, :, cols] = sums[0, o]
+                pot[o, s, :, cols] = sums[1, o]
+            return carry
+
+        lax.fori_loop(0, ny // LANES, block, 0)
+
+    def finish(s):
+        def block(i, carry):
+            cols = pl.ds(pl.multiple_of(i * LANES, LANES), LANES)
+            for o in range(local):
+                own = gathered[slot, o, s, :, cols]
+                pot[o, s, :, cols] = pot[o, s, :, cols] + part_in[o, s, :, cols] + own * own * own
+            return carry
+
+        lax.fori_loop(0, ny // LANES, block, 0)
+
+    def step(t, carry):
+        @pl.when(t < nz)
+        def _():
+            for d in range(inner - 1):
+                x_copy(d, t).wait_recv()
+                f_copy(d, t).start()
+
+        @pl.when(t + DEPTH < nz)
+        def _():
+            send(t + DEPTH)
+
+        @pl.when((t >= 1) & (t < nz + 1))
+        def _():
+            u = t - 1
+            o_copy(u).wait_recv()
+            for d in range(inner - 1):
+                f_copy(d, u).wait_recv()
+            partials(u)
+            y_copy(u).start()
+
+        @pl.when(t >= LAG)
+        def _():
+            v = t - LAG
+            y_copy(v).wait_recv()
+            finish(v)
+            out_copy(v).start()
+
+        return carry
+
+    lax.fori_loop(0, nz + LAG, step, 0)
+
+    def drain(s, carry):
+        for d in range(inner - 1):
+            x_copy(d, s).wait_send()
+            f_copy(d, s).wait_send()
+        o_copy(s).wait_send()
+        y_copy(s).wait_send()
+        out_copy(s).wait()
+        return carry
+
+    lax.fori_loop(0, nz, drain, 0)
+
+
+def potentials(concentration, phase_labels, hessian):
+    local, nz, nx, ny = concentration.shape
+    inner = lax.axis_size("comp") // 4
+    full = (local, nz, nx, ny)
+    dma = pltpu.SemaphoreType.DMA
+    return pl.pallas_call(
+        functools.partial(potential_kernel, inner),
+        out_shape=jax.ShapeDtypeStruct(full, jnp.float32),
+        in_specs=[
+            pl.BlockSpec(memory_space=pl.ANY),
+            pl.BlockSpec(memory_space=pl.ANY),
+            pl.BlockSpec(memory_space=pltpu.SMEM),
+        ],
+        out_specs=pl.BlockSpec(memory_space=pl.ANY),
+        scratch_shapes=[
+            pltpu.VMEM((2 * inner,) + full, jnp.float32),
+            pltpu.VMEM((nz, nx, ny), jnp.int32),
+            pltpu.VMEM(full, jnp.float32),
+            pltpu.VMEM(full, jnp.float32),
+            pltpu.VMEM(full, jnp.float32),
+            dma((inner - 1, nz)), dma((inner - 1, nz)),
+            dma((nz,)), dma((nz,)),
+            dma((inner - 1, nz)), dma((inner - 1, nz)),
+            dma((nz,)), dma((nz,)),
+            dma, dma, dma((nz,)),
+        ],
+        compiler_params=pltpu.CompilerParams(
+            collective_id=0, has_side_effects=True, vmem_limit_bytes=48 * 2**20
+        ),
+    )(concentration, phase_labels, hessian)
 
 
 def on_device(concentration, phase_labels, hessian, mobility):
     local_comps = concentration.shape[0]
     comp_rank = lax.axis_index("comp")
-    col_block = lax.dynamic_slice_in_dim(hessian, comp_rank * local_comps, local_comps, 2)
-    potential = lax.psum_scatter(
-        apply_hessian(col_block, concentration, phase_labels),
-        "comp",
-        scatter_dimension=0,
-        tiled=True,
-    )
-    potential = potential + concentration * concentration * concentration
+    potential = potentials(concentration, phase_labels, hessian)
     own_mobility = lax.dynamic_slice_in_dim(mobility, comp_rank * local_comps, local_comps, 1)
     mobile = jnp.zeros(concentration.shape, jnp.float32)
     for phase in range(own_mobility.shape[0]):

time: 642 us -> 334 us (0.52)
  waiting for transfers between devices: 264 us -> 41.9 us
  matrix products: 161 us -> 0 us
  Pallas kernels: 0 us -> 112 us
  local copies, waits for them, and re-layouts: 98.7 us -> 75.7 us
  between operations: 14.8 us -> 1.22 us
    reduce_scatter x1 -> x0, waiting for transfers between devices: 207 us -> none  [on_device(): lax.psum_scatter(apply_hessian(col_block, concentration, phase_labels), '...]
    dot_general x4 -> x0, matrix products: 161 us -> none  [apply_hessian(): jnp.einsum('ij,jzxy->izxy', tables[phase], fields, precision=lax.Precisio...]
    pallas_call x0 -> x1, Pallas kernels: none -> 112 us  [potentials(): pl.pallas_call(functools.partial(potential_kernel, inner), out_shape=jax....]
    add x1 -> x0, local copies, waits for them, and re-layouts: 31.9 us -> none  [apply_hessian(): summed = summed + jnp.where(phase_map == phase, product, 0.0)]
    ppermute x3, waiting for transfers between devices: 30.4 us -> 17 us  [extended(): after = lax.ppermute(initial, axis, down)]
  transfers between devices with their start and end apart: 7 -> 6, of which waited for: 7 -> 4; matrix products, arithmetic and copies ran while one was open for 0% -> 4% of each run, Pallas kernels for 0% -> 0%
where the time goes in v1:
time: 334 us; the launch traced here: 327 us
  Pallas kernels  112 us (34%)
  other arithmetic  84.6 us (25%)
  local copies, waits for them, and re-layouts  75.7 us (23%)
  waiting for transfers between devices  41.9 us (13%)
  starting transfers between devices  12.1 us (4%)
    pallas_call x1, Pallas kernels, potentials(): pl.pallas_call(functools.partial(potential_kernel, inner), out_shape=jax....  112 us
    add x2, other arithmetic, on_device(): iterate + damping * (source - iterate - bilap_coef * laplace_inner(laplac...  34.4 us
    slice x8, local copies, waits for them, and re-layouts, laplace_inner(): summed = summed + jnp.roll(centre, 1, 3) + jnp.roll(centre, -1, 3)  34 us
    sub x2, other arithmetic, laplace_inner(): return summed - 6.0 * centre  28.7 us
    slice x8, local copies, waits for them, and re-layouts, laplace_inner(): summed = summed + jnp.roll(centre, 1, 1) + jnp.roll(centre, -1, 1)  25.9 us
    ppermute x3, waiting for transfers between devices, extended(): before = lax.ppermute(last, axis, up)  24.9 us
    ppermute x3, waiting for transfers between devices, extended(): after = lax.ppermute(initial, axis, down)  17 us
    add x1, other arithmetic, on_device(): source = concentration + time_step * mobile * laplace_inner(padded)  13.8 us
  transfers between devices with their start and end apart: 6, of which 4 were waited for; matrix products, arithmetic and copies ran while one was open for 4% of the time, Pallas kernels for 0%

profile of v1, /device:TPU:0, one launch (start us, length us, event | category | flops | bytes accessed | tf_op | source)
XLA Modules:
  0.0 327.4 jit_solution(11019155124728888674)
XLA Ops:
  0.6 0.0 copy-start
  0.7 1.6 copy-done.2
  2.2 0.8 copy-done.3
  3.0 111.9 %shard_map.59 = f32[2,16,16,2048]{3,2,1,0:T(8,128)} custom-call(f32[2,16,16,2048]{3,2,1,0:T(8,128)} %c_hbm.1, s32[16,16,2048]{2,1,0:T(8,128)S(1)} %copy-done.2, f32[4,16,16]{2,1,0:T(8,128)S(1)} %copy-done.3), custom_call_target="tpu_custom_call" | custom-call | tf_op jit(solution)/shard_map/pallas_call | solution.py:192
  114.9 3.5 %fusion.65 = (f32[2,16,1,2048]{3,2,1,0:T(1,128)}, f32[2,16,1,2048]{3,2,1,0:T(1,128)S(1)}) fusion(f32[2,16,16,2048]{3,2,1,0:T(8,128)} %shard_map.59), kind=kLoop, calls=%fused_computation.104 | loop fusion | bytes 1048576 | tf_op jit(solution)/shard_map/slice | solution.py:29
  118.4 3.6 %collective-permute-start = (f32[2,16,1,2048]{3,2,1,0:T(1,128)}, f32[2,16,1,2048]{3,2,1,0:T(1,128)S(1)}, u32[]{:S(2)}, u32[]{:S(2)}) collective-permute-start(f32[2,16,1,2048]{3,2,1,0:T(1,128)} %get-tuple-element.38), channel_id=1, source_target_pairs={{1,0},{2,1},{3,2},{0,3},{5,4},{6,5},{7,6},{4,7},{9,8},{10,9},{11,1... | collective-permute-start | bytes 786440 | tf_op jit(solution)/shard_map/ppermute | solution.py:31
  122.0 0.0 collective-permute-start.1
  122.0 1.3 broadcast_compare_fusion.3
  123.4 4.1 %fusion.61 = (f32[2,15,16,2048]{3,2,1,0:T(8,128)}, f32[2,15,16,2048]{3,2,1,0:T(8,128)}) fusion(f32[2,16,16,2048]{3,2,1,0:T(8,128)S(1)} %copy-done.4), kind=kLoop, calls=%fused_computation.100 | loop fusion | bytes 15728640 | tf_op jit(solution)/shard_map/jit(_roll_static)/slice | solution.py:40
  127.5 5.0 %fusion.63 = (f32[2,16,16,2047]{3,2,1,0:T(8,128)}, f32[2,16,16,2047]{3,2,1,0:T(8,128)}) fusion(f32[2,16,16,2048]{3,2,1,0:T(8,128)S(1)} %copy-done.4), kind=kLoop, calls=%fused_computation.102 | loop fusion | bytes 16769024 | tf_op jit(solution)/shard_map/jit(_roll_static)/slice | solution.py:39
  132.4 0.1 constant_dynamic-slice_fusion
  132.5 1.2 fusion.64
  133.7 0.0 collective-permute-done
  133.7 0.0 collective-permute-done.1
  133.7 13.8 %fusion.45 = f32[2,16,16,2048]{3,2,1,0:T(8,128)S(1)} fusion(f32[2,16,16,2048]{3,2,1,0:T(8,128)} %c_hbm.1, f32[2,16,16,2048]{3,2,1,0:T(8,128)} %shard_map.59, f32[2,16,1,2048]{3,2,1,0:T(1,128)S(1)} %collective-permute-done.1, f32[2,16,1,2048]{3,2,1,0:T(1,128)S(1)} %collective-permute-done, f32[2,16,16,2047]{3,2,1,0:T(8,128)} %get-tuple-element.35, ...), kind=kLoop, calls=%fused_computation.72 | loop fusion | flops 24117248 | bytes 31981600 | tf_op jit(solution)/shard_map/add | solution.py:230
  147.5 0.0 copy-start.7
  147.5 0.5 fusion.60
  148.0 1.3 collective-permute-start.3
  149.3 3.2 collective-permute-start.2
  152.4 12.3 %collective-permute-done.3 = f32[2,16,2,2048]{3,2,1,0:T(2,128)S(1)} collective-permute-done((f32[2,16,2,2048]{3,2,1,0:T(2,128)S(1)}, f32[2,16,2,2048]{3,2,1,0:T(2,128)S(1)}, u32[]{:S(2)}, u32[]{:S(2)}) %collective-permute-start.3) | collective-permute-done | bytes 524320 | tf_op jit(solution)/shard_map/ppermute | solution.py:30
  164.7 7.8 %collective-permute-done.2 = f32[2,16,2,2048]{3,2,1,0:T(2,128)S(1)} collective-permute-done((f32[2,16,2,2048]{3,2,1,0:T(2,128)S(1)}, f32[2,16,2,2048]{3,2,1,0:T(2,128)S(1)}, u32[]{:S(2)}, u32[]{:S(2)}) %collective-permute-start.2) | collective-permute-done | bytes 524320 | tf_op jit(solution)/shard_map/ppermute | solution.py:31
  172.5 0.8 copy-done.23
  173.3 3.2 pad_maximum_fusion.16
  176.6 5.7 %fusion.57 = (f32[2,15,18,2048]{3,2,1,0:T(8,128)}, f32[2,15,18,2048]{3,2,1,0:T(8,128)}) fusion(f32[2,16,20,2048]{3,2,1,0:T(8,128)S(1)} %pad_maximum_fusion.16), kind=kLoop, calls=%fused_computation.96 | loop fusion | bytes 17694720 | tf_op jit(solution)/shard_map/jit(_roll_static)/slice | solution.py:40
  182.3 7.8 %fusion.58 = (f32[2,16,18,2047]{3,2,1,0:T(8,128)}, f32[2,16,18,2047]{3,2,1,0:T(8,128)}) fusion(f32[2,16,20,2048]{3,2,1,0:T(8,128)S(1)} %pad_maximum_fusion.16), kind=kLoop, calls=%fused_computation.97 | loop fusion | bytes 18865152 | tf_op jit(solution)/shard_map/jit(_roll_static)/slice | solution.py:39
  190.1 14.3 %fusion.9 = f32[2,16,18,2048]{3,2,1,0:T(8,128)S(1)} fusion(f32[2,16,20,2048]{3,2,1,0:T(8,128)S(1)} %pad_maximum_fusion.16, f32[2,16,2,2048]{3,2,1,0:T(2,128)} %copy-done.23, f32[2,16,16,2048]{3,2,1,0:T(8,128)} %copy-done.7, f32[2,16,2,2048]{3,2,1,0:T(2,128)} %copy-done.21, f32[2,16,18,2047]{3,2,1,0:T(8,128)} %get-tuple-element.25, ...), kind=kLoop, calls=%fused_computation.19 | loop fusion | flops 24772608 | bytes 32960000 | tf_op jit(solution)/shard_map/sub | solution.py:41
  204.4 1.0 fusion.56
  205.5 1.4 fusion.54
  206.9 4.3 %fusion.53 = (f32[2,15,16,2048]{3,2,1,0:T(8,128)}, f32[2,15,16,2048]{3,2,1,0:T(8,128)}) fusion(f32[2,16,18,2048]{3,2,1,0:T(8,128)S(1)} %fusion.9), kind=kLoop, calls=%fused_computation.92 | loop fusion | bytes 15728640 | tf_op jit(solution)/shard_map/jit(_roll_static)/slice | solution.py:40
  211.2 5.6 %fusion.55 = (f32[2,16,16,2047]{3,2,1,0:T(8,128)}, f32[2,16,16,2047]{3,2,1,0:T(8,128)}) fusion(f32[2,16,18,2048]{3,2,1,0:T(8,128)S(1)} %fusion.9), kind=kLoop, calls=%fused_computation.94 | loop fusion | bytes 16769024 | tf_op jit(solution)/shard_map/jit(_roll_static)/slice | solution.py:39
  216.8 16.2 %fusion.33 = f32[2,16,16,2048]{3,2,1,0:T(8,128)} fusion(f32[2,16,16,2048]{3,2,1,0:T(8,128)S(1)} %copy-done.8, f32[2,16,18,2048]{3,2,1,0:T(8,128)} %copy-done.5, f32[2,16,16,2047]{3,2,1,0:T(8,128)} %get-tuple-element.19, f32[2,16,16,1]{3,2,1,0:T(8,128)} %get-tuple-element.21, f32[2,16,16,1]{3,2,1,0:T(8,128)S(1)} %get-tuple-element.20, ...), kind=kLoop, calls=%fused_computation.58 | loop fusion | flops 28311552 | bytes 39845920 | tf_op jit(solution)/shard_map/add | solution.py:237
  233.0 2.7 fusion.59
  235.7 1.6 collective-permute-start.5
  237.2 2.5 collective-permute-start.4
  239.7 12.7 %collective-permute-done.5 = f32[2,16,2,2048]{3,2,1,0:T(2,128)S(1)} collective-permute-done((f32[2,16,2,2048]{3,2,1,0:T(2,128)S(1)}, f32[2,16,2,2048]{3,2,1,0:T(2,128)S(1)}, u32[]{:S(2)}, u32[]{:S(2)}) %collective-permute-start.5) | collective-permute-done | bytes 524320 | tf_op jit(solution)/shard_map/ppermute | solution.py:30
  252.4 9.1 %collective-permute-done.4 = f32[2,16,2,2048]{3,2,1,0:T(2,128)S(1)} collective-permute-done((f32[2,16,2,2048]{3,2,1,0:T(2,128)S(1)}, f32[2,16,2,2048]{3,2,1,0:T(2,128)S(1)}, u32[]{:S(2)}, u32[]{:S(2)}) %collective-permute-start.4) | collective-permute-done | bytes 524320 | tf_op jit(solution)/shard_map/ppermute | solution.py:31
  261.6 0.8 copy-done.24
  262.4 3.2 pad_maximum_fusion.17
  265.6 5.7 %fusion.51 = (f32[2,15,18,2048]{3,2,1,0:T(8,128)}, f32[2,15,18,2048]{3,2,1,0:T(8,128)}) fusion(f32[2,16,20,2048]{3,2,1,0:T(8,128)S(1)} %pad_maximum_fusion.17), kind=kLoop, calls=%fused_computation.90 | loop fusion | bytes 17694720 | tf_op jit(solution)/shard_map/jit(_roll_static)/slice | solution.py:40
  271.3 7.8 %fusion.52 = (f32[2,16,18,2047]{3,2,1,0:T(8,128)}, f32[2,16,18,2047]{3,2,1,0:T(8,128)}) fusion(f32[2,16,20,2048]{3,2,1,0:T(8,128)S(1)} %pad_maximum_fusion.17), kind=kLoop, calls=%fused_computation.91 | loop fusion | bytes 18865152 | tf_op jit(solution)/shard_map/jit(_roll_static)/slice | solution.py:39
  279.2 14.4 %fusion = f32[2,16,18,2048]{3,2,1,0:T(8,128)S(1)} fusion(f32[2,16,20,2048]{3,2,1,0:T(8,128)S(1)} %pad_maximum_fusion.17, f32[2,16,2,2048]{3,2,1,0:T(2,128)} %copy-done.24, f32[2,16,16,2048]{3,2,1,0:T(8,128)} %fusion.33, f32[2,16,2,2048]{3,2,1,0:T(2,128)} %copy-done.22, f32[2,16,18,2047]{3,2,1,0:T(8,128)} %get-tuple-element.13, ...), kind=kLoop, calls=%fused_computation.1 | loop fusion | flops 24772608 | bytes 32960000 | tf_op jit(solution)/shard_map/sub | solution.py:41
  293.6 0.2 fusion.50
  293.8 4.6 %fusion.47 = (f32[2,15,16,2048]{3,2,1,0:T(8,128)}, f32[2,15,16,2048]{3,2,1,0:T(8,128)}) fusion(f32[2,16,18,2048]{3,2,1,0:T(8,128)S(1)} %fusion), kind=kLoop, calls=%fused_computation.86 | loop fusion | bytes 15728640 | tf_op jit(solution)/shard_map/jit(_roll_static)/slice | solution.py:40
  298.4 0.3 copy-done.6
  298.6 5.5 %fusion.49 = (f32[2,16,16,2047]{3,2,1,0:T(8,128)}, f32[2,16,16,2047]{3,2,1,0:T(8,128)}) fusion(f32[2,16,18,2048]{3,2,1,0:T(8,128)S(1)} %fusion), kind=kLoop, calls=%fused_computation.88 | loop fusion | bytes 16769024 | tf_op jit(solution)/shard_map/jit(_roll_static)/slice | solution.py:39
  304.1 0.0 copy-start.1
  304.1 18.3 %fusion.23 = f32[2,16,16,2048]{3,2,1,0:T(8,128)} fusion(f32[2,16,16,2048]{3,2,1,0:T(8,128)} %fusion.33, f32[2,16,18,2048]{3,2,1,0:T(8,128)} %copy-done.6, f32[2,16,16,2047]{3,2,1,0:T(8,128)} %get-tuple-element.7, f32[2,16,16,1]{3,2,1,0:T(8,128)S(1)} %get-tuple-element.9, f32[2,16,16,1]{3,2,1,0:T(8,128)S(1)} %get-tuple-element.8, ...), kind=kLoop, calls=%fused_computation.46 | loop fusion | flops 28311552 | bytes 44040224 | tf_op jit(solution)/shard_map/add | solution.py:237
  322.4 4.7 %copy.7 = f32[2,16,16,2048]{3,2,1,0:T(8,128)} copy(f32[2,16,16,2048]{3,2,1,0:T(8,128)} %shard_map.59) | data formatting | bytes 8388608
  (45 shorter events, 0.2 us)
Async XLA Ops:
  0.6 131.8 %copy-start = (f32[4,16]{1,0:T(4,128)S(1)}, f32[4,16]{1,0:T(4,128)}, u32[]{:S(2)}) copy-start(f32[4,16]{1,0:T(4,128)} %param.7) | copy-start | bytes 772
  0.6 1.6 copy-start.2
  2.2 0.8 copy-start.3
  114.9 8.4 %copy-start.4 = (f32[2,16,16,2048]{3,2,1,0:T(8,128)S(1)}, f32[2,16,16,2048]{3,2,1,0:T(8,128)}, u32[]{:S(2)}) copy-start(f32[2,16,16,2048]{3,2,1,0:T(8,128)} %shard_map.59) | copy-start | bytes 12582916
  118.4 15.2 %collective-permute-start = (f32[2,16,1,2048]{3,2,1,0:T(1,128)}, f32[2,16,1,2048]{3,2,1,0:T(1,128)S(1)}, u32[]{:S(2)}, u32[]{:S(2)}) collective-permute-start(f32[2,16,1,2048]{3,2,1,0:T(1,128)} %get-tuple-element.38), channel_id=1, source_target_pairs={{1,0},{2,1},{3,2},{0,3},{5,4},{6,5},{7,6},{4,7},{9,8},{10,9},{11,1... | collective-permute-start | bytes 786440 | tf_op jit(solution)/shard_map/ppermute | solution.py:31
  122.0 11.7 %collective-permute-start.1 = (f32[2,16,1,2048]{3,2,1,0:T(1,128)S(1)}, f32[2,16,1,2048]{3,2,1,0:T(1,128)S(1)}, u32[]{:S(2)}, u32[]{:S(2)}) collective-permute-start(f32[2,16,1,2048]{3,2,1,0:T(1,128)S(1)} %get-tuple-element.39), channel_id=1, source_target_pairs={{0,1},{1,2},{2,3},{3,0},{4,5},{5,6},{6,7},{7,4},{8,9},{9,10},{10,1... | collective-permute-start | bytes 786440 | tf_op jit(solution)/shard_map/ppermute | solution.py:30
  123.3 10.4 %copy-start.9 = (pred[16,16,2048]{2,1,0:T(8,128)(4,1)}, pred[16,16,2048]{2,1,0:T(8,128)(4,1)S(1)}, u32[]{:S(2)}) copy-start(pred[16,16,2048]{2,1,0:T(8,128)(4,1)S(1)} %get-tuple-element.40) | copy-start | bytes 1572868
  123.3 10.4 %copy-start.12 = (pred[16,16,2048]{2,1,0:T(8,128)(4,1)}, pred[16,16,2048]{2,1,0:T(8,128)(4,1)S(1)}, u32[]{:S(2)}) copy-start(pred[16,16,2048]{2,1,0:T(8,128)(4,1)S(1)} %get-tuple-element.41) | copy-start | bytes 1572868
  123.3 10.4 %copy-start.15 = (pred[16,16,2048]{2,1,0:T(8,128)(4,1)}, pred[16,16,2048]{2,1,0:T(8,128)(4,1)S(1)}, u32[]{:S(2)}) copy-start(pred[16,16,2048]{2,1,0:T(8,128)(4,1)S(1)} %get-tuple-element.42) | copy-start | bytes 1572868
  123.3 10.4 %copy-start.18 = (pred[16,16,2048]{2,1,0:T(8,128)(4,1)}, pred[16,16,2048]{2,1,0:T(8,128)(4,1)S(1)}, u32[]{:S(2)}) copy-start(pred[16,16,2048]{2,1,0:T(8,128)(4,1)S(1)} %get-tuple-element.43) | copy-start | bytes 1572868
  147.5 17.2 %copy-start.7 = (f32[2,16,16,2048]{3,2,1,0:T(8,128)}, f32[2,16,16,2048]{3,2,1,0:T(8,128)S(1)}, u32[]{:S(2)}) copy-start(f32[2,16,16,2048]{3,2,1,0:T(8,128)S(1)} %fusion.45) | copy-start | bytes 12582916
  148.0 16.7 %collective-permute-start.3 = (f32[2,16,2,2048]{3,2,1,0:T(2,128)S(1)}, f32[2,16,2,2048]{3,2,1,0:T(2,128)S(1)}, u32[]{:S(2)}, u32[]{:S(2)}) collective-permute-start(f32[2,16,2,2048]{3,2,1,0:T(2,128)S(1)} %get-tuple-element.28), channel_id=1, source_target_pairs={{0,1},{1,2},{2,3},{3,0},{4,5},{5,6},{6,7},{7,4},{8,9},{9,10},{10,1... | collective-permute-start | bytes 1572872 | tf_op jit(solution)/shard_map/ppermute | solution.py:30
  149.3 23.3 %collective-permute-start.2 = (f32[2,16,2,2048]{3,2,1,0:T(2,128)S(1)}, f32[2,16,2,2048]{3,2,1,0:T(2,128)S(1)}, u32[]{:S(2)}, u32[]{:S(2)}) collective-permute-start(f32[2,16,2,2048]{3,2,1,0:T(2,128)S(1)} %get-tuple-element.29), channel_id=1, source_target_pairs={{1,0},{2,1},{3,2},{0,3},{5,4},{6,5},{7,6},{4,7},{9,8},{10,9},{11,1... | collective-permute-start | bytes 1572872 | tf_op jit(solution)/shard_map/ppermute | solution.py:31
  164.7 7.8 %copy-start.21 = (f32[2,16,2,2048]{3,2,1,0:T(2,128)}, f32[2,16,2,2048]{3,2,1,0:T(2,128)S(1)}, u32[]{:S(2)}) copy-start(f32[2,16,2,2048]{3,2,1,0:T(2,128)S(1)} %collective-permute-done.3) | copy-start | bytes 1572868
  172.5 0.8 copy-start.23
  204.4 6.7 %copy-start.5 = (f32[2,16,18,2048]{3,2,1,0:T(8,128)}, f32[2,16,18,2048]{3,2,1,0:T(8,128)S(1)}, u32[]{:S(2)}) copy-start(f32[2,16,18,2048]{3,2,1,0:T(8,128)S(1)} %fusion.9) | copy-start | bytes 14155780
  211.2 5.6 %copy-start.8 = (f32[2,16,16,2048]{3,2,1,0:T(8,128)S(1)}, f32[2,16,16,2048]{3,2,1,0:T(8,128)}, u32[]{:S(2)}) copy-start(f32[2,16,16,2048]{3,2,1,0:T(8,128)} %copy-done.7) | copy-start | bytes 12582916
  211.2 5.6 %copy-start.10 = (pred[16,16,2048]{2,1,0:T(8,128)(4,1)S(1)}, pred[16,16,2048]{2,1,0:T(8,128)(4,1)}, u32[]{:S(2)}) copy-start(pred[16,16,2048]{2,1,0:T(8,128)(4,1)} %copy-done.9) | copy-start | bytes 1572868
  211.2 5.6 %copy-start.13 = (pred[16,16,2048]{2,1,0:T(8,128)(4,1)S(1)}, pred[16,16,2048]{2,1,0:T(8,128)(4,1)}, u32[]{:S(2)}) copy-start(pred[16,16,2048]{2,1,0:T(8,128)(4,1)} %copy-done.12) | copy-start | bytes 1572868
  211.2 5.6 %copy-start.16 = (pred[16,16,2048]{2,1,0:T(8,128)(4,1)S(1)}, pred[16,16,2048]{2,1,0:T(8,128)(4,1)}, u32[]{:S(2)}) copy-start(pred[16,16,2048]{2,1,0:T(8,128)(4,1)} %copy-done.15) | copy-start | bytes 1572868
  211.2 5.6 %copy-start.19 = (pred[16,16,2048]{2,1,0:T(8,128)(4,1)S(1)}, pred[16,16,2048]{2,1,0:T(8,128)(4,1)}, u32[]{:S(2)}) copy-start(pred[16,16,2048]{2,1,0:T(8,128)(4,1)} %copy-done.18) | copy-start | bytes 1572868
  235.7 16.7 %collective-permute-start.5 = (f32[2,16,2,2048]{3,2,1,0:T(2,128)S(1)}, f32[2,16,2,2048]{3,2,1,0:T(2,128)S(1)}, u32[]{:S(2)}, u32[]{:S(2)}) collective-permute-start(f32[2,16,2,2048]{3,2,1,0:T(2,128)S(1)} %get-tuple-element.26), channel_id=1, source_target_pairs={{0,1},{1,2},{2,3},{3,0},{4,5},{5,6},{6,7},{7,4},{8,9},{9,10},{10,1... | collective-permute-start | bytes 1572872 | tf_op jit(solution)/shard_map/ppermute | solution.py:30
  237.2 24.3 %collective-permute-start.4 = (f32[2,16,2,2048]{3,2,1,0:T(2,128)S(1)}, f32[2,16,2,2048]{3,2,1,0:T(2,128)S(1)}, u32[]{:S(2)}, u32[]{:S(2)}) collective-permute-start(f32[2,16,2,2048]{3,2,1,0:T(2,128)S(1)} %get-tuple-element.27), channel_id=1, source_target_pairs={{1,0},{2,1},{3,2},{0,3},{5,4},{6,5},{7,6},{4,7},{9,8},{10,9},{11,1... | collective-permute-start | bytes 1572872 | tf_op jit(solution)/shard_map/ppermute | solution.py:31
  252.4 9.1 %copy-start.22 = (f32[2,16,2,2048]{3,2,1,0:T(2,128)}, f32[2,16,2,2048]{3,2,1,0:T(2,128)S(1)}, u32[]{:S(2)}) copy-start(f32[2,16,2,2048]{3,2,1,0:T(2,128)S(1)} %collective-permute-done.5) | copy-start | bytes 1572868
  261.6 0.8 copy-start.24
  293.5 5.1 %copy-start.6 = (f32[2,16,18,2048]{3,2,1,0:T(8,128)}, f32[2,16,18,2048]{3,2,1,0:T(8,128)S(1)}, u32[]{:S(2)}) copy-start(f32[2,16,18,2048]{3,2,1,0:T(8,128)S(1)} %fusion) | copy-start | bytes 14155780
  298.6 5.5 %copy-start.11 = (pred[16,16,2048]{2,1,0:T(8,128)(4,1)S(1)}, pred[16,16,2048]{2,1,0:T(8,128)(4,1)}, u32[]{:S(2)}) copy-start(pred[16,16,2048]{2,1,0:T(8,128)(4,1)} %copy-done.9) | copy-start | bytes 1572868
  298.6 5.5 %copy-start.14 = (pred[16,16,2048]{2,1,0:T(8,128)(4,1)S(1)}, pred[16,16,2048]{2,1,0:T(8,128)(4,1)}, u32[]{:S(2)}) copy-start(pred[16,16,2048]{2,1,0:T(8,128)(4,1)} %copy-done.12) | copy-start | bytes 1572868
  298.6 5.5 %copy-start.17 = (pred[16,16,2048]{2,1,0:T(8,128)(4,1)S(1)}, pred[16,16,2048]{2,1,0:T(8,128)(4,1)}, u32[]{:S(2)}) copy-start(pred[16,16,2048]{2,1,0:T(8,128)(4,1)} %copy-done.15) | copy-start | bytes 1572868
  298.6 5.5 %copy-start.20 = (pred[16,16,2048]{2,1,0:T(8,128)(4,1)S(1)}, pred[16,16,2048]{2,1,0:T(8,128)(4,1)}, u32[]{:S(2)}) copy-start(pred[16,16,2048]{2,1,0:T(8,128)(4,1)} %copy-done.18) | copy-start | bytes 1572868
  304.1 23.0 %copy-start.1 = (f32[4,16]{1,0:T(4,128)S(1)}, f32[4,16]{1,0:T(4,128)}, u32[]{:S(2)}) copy-start(f32[4,16]{1,0:T(4,128)} %param.7) | copy-start | bytes 772

commit v2 on v1

v2 whole, which is shorter than its diff:
```python
import functools

import jax
import jax.numpy as jnp
from jax import lax
from jax.experimental import pallas as pl
from jax.experimental.pallas import tpu as pltpu
from jax.sharding import PartitionSpec as P

time_step = 0.1
stiff_step = 0.02
damping = 0.5

MESH = pl.DeviceIdType.MESH
DEPTH = 3
LAG = 3
LANES = 256
EDGE = 4


def laplace(field, before, after, above, below):
    summed = before + after + above + below
    summed = summed + pltpu.roll(field, 1, 1) + pltpu.roll(field, field.shape[1] - 1, 1)
    return summed - 6.0 * field


def brick_kernel(
    inner, c_hbm, ph_hbm, h_ref, table, new_hbm, pot_hbm,
    gathered, labels, part_out, part_in, pot, source, twice, first,
    label_out, label_in, pot_out, pot_in, src_out, src_in,
    xs, xr, os, orr, fs, fr, ys, yr, own_sem, label_sem, out_sem, new_sem,
    ls, lr, ps, pr, ss, sr,
):
    local, nz, nx, ny = c_hbm.shape
    phases = h_ref.shape[0]
    me = lax.axis_index("comp")
    core = lax.rem(me, 2)
    spot = lax.rem(me // 2, inner)
    row = me // (2 * inner)

    def index(a, b, k):
        return (a * inner + b) * 2 + k

    sibling = index(row, spot, 1 - core)
    across = index(1 - row, spot, core)
    slot = spot * 2 + core
    peers = [index(row, lax.rem(spot + d, inner), core) for d in range(1, inner)]
    sources = [lax.rem(spot + inner - d, inner) * 2 + core for d in range(1, inner)]

    def remote(src, dst, send, recv, device):
        return pltpu.make_async_remote_copy(
            src_ref=src, dst_ref=dst, send_sem=send, recv_sem=recv,
            device_id={"comp": device}, device_id_type=MESH,
        )

    place_x = lax.axis_index("space")
    bricks = lax.axis_size("space")
    beside = (lax.rem(place_x + 1, bricks), lax.rem(place_x + bricks - 1, bricks))

    def aside(src, dst, send, recv, side):
        return pltpu.make_async_remote_copy(
            src_ref=src, dst_ref=dst, send_sem=send, recv_sem=recv,
            device_id={"space": beside[side]}, device_id_type=MESH,
        )

    def x_copy(d, s):
        return remote(c_hbm.at[:, s], gathered.at[slot, :, s], xs.at[d, s], xr.at[d, s], peers[d])

    def o_copy(s):
        return remote(c_hbm.at[:, s], gathered.at[slot, :, s], os.at[s], orr.at[s], sibling)

    def f_copy(d, s):
        place = gathered.at[sources[d], :, s]
        return remote(place, place, fs.at[d, s], fr.at[d, s], sibling)

    def y_copy(s):
        return remote(part_out.at[:, s], part_in.at[:, s], ys.at[s], yr.at[s], across)

    def l_copy(side):
        return aside(label_out.at[side], label_in.at[side], ls.at[side], lr.at[side], side)

    def p_copy(side, s):
        return aside(pot_out.at[side, :, s], pot_in.at[side, :, s], ps.at[side, s], pr.at[side, s], side)

    def s_copy(side, s):
        return aside(src_out.at[side, :, s], src_in.at[side, :, s], ss.at[side, s], sr.at[side, s], side)

    def new_copy(s):
        return pltpu.make_async_copy(part_in.at[:, s], new_hbm.at[:, s], new_sem.at[s])

    def out_copy(s):
        return pltpu.make_async_copy(pot.at[:, s], pot_hbm.at[:, s], out_sem.at[s])

    own_copy = pltpu.make_async_copy(c_hbm, gathered.at[slot], own_sem)
    label_copy = pltpu.make_async_copy(ph_hbm, labels.at[:, 0:nx], label_sem)
    own_copy.start()
    label_copy.start()

    barrier = pltpu.get_barrier_semaphore()
    others = peers + [sibling, across]
    for other in others:
        pl.semaphore_signal(barrier, inc=1, device_id={"comp": other}, device_id_type=MESH)
    for brick in beside:
        pl.semaphore_signal(barrier, inc=1, device_id={"space": brick}, device_id_type=MESH)
    pl.semaphore_wait(barrier, len(others) + 2)

    def send(s):
        for d in range(inner - 1):
            x_copy(d, s).start()
        o_copy(s).start()

    for s in range(min(DEPTH, nz)):
        send(s)
    own_copy.wait()
    label_copy.wait()

    def label_edges(z, carry):
        label_out[0, z] = labels[z, nx - EDGE : nx, :]
        label_out[1, z] = labels[z, 0:EDGE, :]
        return carry

    lax.fori_loop(0, nz, label_edges, 0)
    l_copy(0).start()
    l_copy(1).start()

    def partials(s):
        def block(i, carry):
            cols = pl.ds(pl.multiple_of(i * LANES, LANES), LANES)
            phase = labels[s, 0:nx, cols]
            masks = [phase == p for p in range(1, phases)]
            sums = {}
            for j in range(2 * inner):
                for l in range(local):
                    value = gathered[j, l, s, :, cols]
                    column = (row * 2 * inner + j) * local + l
                    for side, owner in enumerate((across, me)):
                        for o in range(local):
                            line = owner * local + o
                            factor = h_ref[0, line, column]
                            for p in range(1, phases):
                                factor = jnp.where(masks[p - 1], h_ref[p, line, column], factor)
                            term = factor * value
                            key = (side, o)
                            sums[key] = sums[key] + term if key in sums else term
            for o in range(local):
                part_out[o, s, :, cols] = sums[0, o]
                pot[o, s, :, cols] = sums[1, o]
            return carry

        lax.fori_loop(0, ny // LANES, block, 0)

    def finish(s):
        def block(i, carry):
            cols = pl.ds(pl.multiple_of(i * LANES, LANES), LANES)
            for o in range(local):
                own = gathered[slot, o, s, :, cols]
                pot[o, s, :, cols] = pot[o, s, :, cols] + part_in[o, s, :, cols] + own * own * own
            return carry

        lax.fori_loop(0, ny // LANES, block, 0)
        for o in range(local):
            pot_out[0, o, s] = pot[o, s, nx - 1 : nx, :]
            pot_out[1, o, s] = pot[o, s, 0:1, :]

    def plane(z):
        return lax.rem(z, nz)

    def chosen(kind, l, phase):
        result = table[kind, 0, me * local + l]
        for p in range(1, phases):
            result = jnp.where(phase == p, table[kind, p, me * local + l], result)
        return result

    def make_source(z):
        now, low, high = plane(z), plane(z + nz - 1), plane(z + 1)
        for side in range(2):
            p_copy(side, now).wait_recv()

        def component(l, carry):
            field = pot[l, now]
            line = lax.broadcasted_iota(jnp.int32, field.shape, 0)
            before = jnp.where(line == 0, pot_in[0, l, now], pltpu.roll(field, 1, 0))
            after = jnp.where(line == nx - 1, pot_in[1, l, now], pltpu.roll(field, nx - 1, 0))
            lap = laplace(field, before, after, pot[l, low], pot[l, high])
            value = gathered[slot, l, now] + chosen(0, l, labels[now, 0:nx, :]) * lap
            source[l, now, 0:nx, :] = value
            src_out[0, l, now] = value[nx - EDGE : nx]
            src_out[1, l, now] = value[0:EDGE]
            return carry

        lax.fori_loop(0, local, component, 0)
        for side in range(2):
            s_copy(side, now).start()

    def take_edges(z):
        now = plane(z)
        for side in range(2):
            s_copy(side, now).wait_recv()
        for l in range(local):
            source[l, now, nx : nx + EDGE, :] = src_in[1, l, now]
            source[l, now, nx + EDGE : nx + 2 * EDGE, :] = src_in[0, l, now]

    def once(ref, l, z, rows):
        now, low, high = plane(z), plane(z + nz - 1), plane(z + 1)
        field = ref[l, now]
        before = pltpu.roll(field, 1, 0)
        after = pltpu.roll(field, field.shape[0] - 1, 0)
        cut = slice(0, rows)
        return laplace(field[cut], before[cut], after[cut], ref[l, low, cut, :], ref[l, high, cut, :])

    wide = nx + 2 * EDGE

    def half(ref, z):
        def component(l, carry):
            twice[l, plane(z)] = once(ref, l, z, wide)
            return carry

        lax.fori_loop(0, local, component, 0)

    def sweep(ref, z, rows, store):
        now = plane(z)

        def component(l, carry):
            phase = labels[now, 0:rows, :]
            old = ref[l, now, 0:rows, :]
            bend = chosen(1, l, phase) * once(twice, l, z, rows)
            store[l, now] = old + chosen(2, l, phase) * (source[l, now, 0:rows, :] - old - bend)
            return carry

        lax.fori_loop(0, local, component, 0)

    def step(t, carry):
        @pl.when(t < nz)
        def _():
            for d in range(inner - 1):
                x_copy(d, t).wait_recv()
                f_copy(d, t).start()

        @pl.when(t + DEPTH < nz)
        def _():
            send(t + DEPTH)

        @pl.when((t >= 1) & (t < nz + 1))
        def _():
            u = t - 1
            o_copy(u).wait_recv()
            for d in range(inner - 1):
                f_copy(d, u).wait_recv()
            partials(u)
            y_copy(u).start()

        @pl.when((t >= LAG) & (t < nz + LAG))
        def _():
            v = t - LAG
            y_copy(v).wait_recv()
            finish(v)
            out_copy(v).start()
            for side in range(2):
                p_copy(side, v).start()

        @pl.when(t == LAG)
        def _():
            for side in range(2):
                l_copy(side).wait_recv()

            def widen(z, carry):
                labels[z, nx : nx + EDGE, :] = label_in[1, z]
                labels[z, nx + EDGE : nx + 2 * EDGE, :] = label_in[0, z]
                return carry

            lax.fori_loop(0, nz, widen, 0)

        w = t - LAG - 2

        @pl.when((w >= 1) & (w < nz + 1))
        def _():
            make_source(w)

        @pl.when((w - 2 >= 1) & (w - 2 < nz + 1))
        def _():
            take_edges(w - 2)

        @pl.when((w - 3 >= 2) & (w - 3 < nz + 2))
        def _():
            half(source, w - 3)

        @pl.when((w - 4 >= 3) & (w - 4 < nz + 3))
        def _():
            sweep(source, w - 4, wide, first)

        @pl.when((w - 5 >= 4) & (w - 5 < nz + 4))
        def _():
            half(first, w - 5)

        @pl.when(w - 6 >= 5)
        def _():
            sweep(first, w - 6, nx, part_in)
            new_copy(plane(w - 6)).start()

        return carry

    lax.fori_loop(0, nz + 5 + LAG + 8, step, 0)
    for side in range(2):
        l_copy(side).wait_send()

    def drain(s, carry):
        for d in range(inner - 1):
            x_copy(d, s).wait_send()
            f_copy(d, s).wait_send()
        o_copy(s).wait_send()
        y_copy(s).wait_send()
        out_copy(s).wait()
        new_copy(s).wait()
        for side in range(2):
            p_copy(side, s).wait_send()
            s_copy(side, s).wait_send()
        return carry

    lax.fori_loop(0, nz, drain, 0)


def on_device(concentration, phase_labels, hessian, mobility):
    local, nz, nx, ny = concentration.shape
    inner = lax.axis_size("comp") // 4
    full = (local, nz, nx, ny)
    wide = (local, nz, nx + 2 * EDGE, ny)
    coef = stiff_step * mobility
    table = jnp.stack([time_step * mobility, coef, damping / (1.0 + 42.0 * coef)])
    dma = pltpu.SemaphoreType.DMA
    f32 = jnp.float32
    return pl.pallas_call(
        functools.partial(brick_kernel, inner),
        out_shape=[jax.ShapeDtypeStruct(full, f32)] * 2,
        in_specs=[
            pl.BlockSpec(memory_space=pl.ANY),
            pl.BlockSpec(memory_space=pl.ANY),
            pl.BlockSpec(memory_space=pltpu.SMEM),
            pl.BlockSpec(memory_space=pltpu.SMEM),
        ],
        out_specs=[pl.BlockSpec(memory_space=pl.ANY)] * 2,
        scratch_shapes=[
            pltpu.VMEM((2 * inner,) + full, f32),
            pltpu.VMEM(wide[1:], jnp.int32),
            pltpu.VMEM(full, f32),
            pltpu.VMEM(full, f32),
            pltpu.VMEM(full, f32),
            pltpu.VMEM(wide, f32),
            pltpu.VMEM(wide, f32),
            pltpu.VMEM(wide, f32),
            pltpu.VMEM((2, nz, EDGE, ny), jnp.int32),
            pltpu.VMEM((2, nz, EDGE, ny), jnp.int32),
            pltpu.VMEM((2, local, nz, 1, ny), f32),
            pltpu.VMEM((2, local, nz, 1, ny), f32),
            pltpu.VMEM((2, local, nz, EDGE, ny), f32),
            pltpu.VMEM((2, local, nz, EDGE, ny), f32),
            dma((inner - 1, nz)), dma((inner - 1, nz)),
            dma((nz,)), dma((nz,)),
            dma((inner - 1, nz)), dma((inner - 1, nz)),
            dma((nz,)), dma((nz,)),
            dma, dma, dma((nz,)), dma((nz,)),
            dma((2,)), dma((2,)),
            dma((2, nz)), dma((2, nz)), dma((2, nz)), dma((2, nz)),
        ],
        compiler_params=pltpu.CompilerParams(
            collective_id=0, has_side_effects=True, vmem_limit_bytes=60 * 2**20
        ),
    )(concentration, phase_labels, hessian, table)


def solution(mesh):
    in_specs = (P("comp", None, "space", None), P(None, "space", None), P(), P())
    out_specs = (P("comp", None, "space", None), P("comp", None, "space", None))
    return jax.shard_map(
        on_device, mesh=mesh, in_specs=in_specs, out_specs=out_specs, check_vma=False
    )
```

time: 334 us -> 147 us (0.44); the launches traced: 327 us -> 147 us
  other arithmetic: 84.6 us -> 1.29 us
  local copies, waits for them, and re-layouts: 75.7 us -> 6.87 us
  waiting for transfers between devices: 41.9 us -> 0 us
  Pallas kernels: 112 us -> 138 us
  starting transfers between devices: 12.1 us -> 0 us
    slice x19 -> x0, local copies, waits for them, and re-layouts: 66.6 us -> none  [the longest x8 34 us: laplace_inner(): summed = summed + jnp.roll(centre, 1, 3) + jnp.roll(centre, -1, 3)]
    add x3 -> x0, other arithmetic: 48.2 us -> none  [the longest x2 34.4 us: on_device(): iterate + damping * (source - iterate - bilap_coef * laplace_inner(laplac...]
    ppermute x6 -> x0, waiting for transfers between devices: 41.9 us -> none  [the longest x3 24.9 us: extended(): before = lax.ppermute(last, axis, up)]
    sub x2 -> x0, other arithmetic: 28.7 us -> none  [laplace_inner(): return summed - 6.0 * centre]
    pallas_call x1, Pallas kernels: 112 us -> 138 us  [on_device(): pl.pallas_call(functools.partial(brick_kernel, inner), out_shape=[jax.Sha...]
    ppermute x6 -> x0, starting transfers between devices: 12.1 us -> none  [the longest x3 9.29 us: extended(): after = lax.ppermute(initial, axis, down)]
    concatenate x2 -> x0, other arithmetic: 6.48 us -> none  [extended(): shard = jnp.concatenate([before, shard, after], axis=dim)]
    unnamed x51 -> x4, local copies, waits for them, and re-layouts: 8.98 us -> 6.87 us
  transfers between devices with their start and end apart: 6 -> 0, of which waited for: 4 -> 0; matrix products, arithmetic and copies ran while one was open for 4% -> 0% of each run, Pallas kernels for 0% -> 0%
where the time goes in v2:
time: 147 us
  Pallas kernels  138 us (94%)
  local copies, waits for them, and re-layouts  6.87 us (5%)
    pallas_call x1, Pallas kernels, on_device(): pl.pallas_call(functools.partial(brick_kernel, inner), out_shape=[jax.Sha...  138 us
    unnamed x4, local copies, waits for them, and re-layouts  6.87 us

profile of v2, /device:TPU:0, one launch (start us, length us, event | category | flops | bytes accessed | tf_op | source)
XLA Modules:
  0.0 146.5 jit_solution(16652828546366887497)
XLA Ops:
  0.6 0.7 multiply_bitcast_fusion.1
  1.3 0.6 pad_maximum_fusion.table
  1.9 137.7 %shard_map.59 = (f32[2,16,16,2048]{3,2,1,0:T(8,128)}, f32[2,16,16,2048]{3,2,1,0:T(8,128)}) custom-call(f32[2,16,16,2048]{3,2,1,0:T(8,128)} %c_hbm.1, s32[16,16,2048]{2,1,0:T(8,128)} %ph_hbm.1, f32[4,16,16]{2,1,0:T(8,128)} %h_ref.1, f32[3,4,16]{2,1,0:T(4,128)} %pad_maximum_fusion.table), custom_call_target="tpu_custom_call" | custom-call | tf_op jit(solution)/shard_map/pallas_call | solution.py:331
  139.6 0.0 copy-start
  139.6 4.8 %copy.8 = f32[2,16,16,2048]{3,2,1,0:T(8,128)} copy(f32[2,16,16,2048]{3,2,1,0:T(8,128)} %get-tuple-element.7) | data formatting | bytes 8388608
  144.5 0.0 copy-done
  144.5 2.0 %copy.9 = f32[2,16,16,2048]{3,2,1,0:T(8,128)} copy(f32[2,16,16,2048]{3,2,1,0:T(8,128)S(1)} %copy-done) | data formatting | bytes 8388608
Async XLA Ops:
  139.6 4.9 %copy-start = (f32[2,16,16,2048]{3,2,1,0:T(8,128)S(1)}, f32[2,16,16,2048]{3,2,1,0:T(8,128)}, u32[]{:S(2)}) copy-start(f32[2,16,16,2048]{3,2,1,0:T(8,128)} %get-tuple-element.8) | copy-start | bytes 12582916

commit v3 on v2

--- a/solution.py
+++ b/solution.py
@@ -12,8 +12,9 @@
 damping = 0.5
 
 MESH = pl.DeviceIdType.MESH
-DEPTH = 3
-LAG = 3
+PARTS = 2
+DEPTH = 7
+LAG = 5
 LANES = 256
 EDGE = 4
 
@@ -25,10 +26,10 @@
 
 
 def brick_kernel(
-    inner, c_hbm, ph_hbm, h_ref, table, new_hbm, pot_hbm,
-    gathered, labels, part_out, part_in, pot, source, twice, first,
+    inner, c_hbm, ph_hbm, h_ref, table, fresh, pot,
+    gathered, labels, part_out, part_in, source, twice, first,
     label_out, label_in, pot_out, pot_in, src_out, src_in,
-    xs, xr, os, orr, fs, fr, ys, yr, own_sem, label_sem, out_sem, new_sem,
+    xs, xr, os, orr, fs, fr, ys, yr, own_sem, label_sem,
     ls, lr, ps, pr, ss, sr,
 ):
     local, nz, nx, ny = c_hbm.shape
@@ -63,18 +64,30 @@
             device_id={"space": beside[side]}, device_id_type=MESH,
         )
 
+    units = nz * PARTS
+    span = ny // PARTS
+
+    def unit(s):
+        return s // PARTS, pl.ds(pl.multiple_of(lax.rem(s, PARTS) * span, 128), span)
+
     def x_copy(d, s):
-        return remote(c_hbm.at[:, s], gathered.at[slot, :, s], xs.at[d, s], xr.at[d, s], peers[d])
+        z, cols = unit(s)
+        return remote(
+            c_hbm.at[:, z, :, cols], gathered.at[slot, :, z, :, cols], xs.at[d, s], xr.at[d, s], peers[d]
+        )
 
     def o_copy(s):
-        return remote(c_hbm.at[:, s], gathered.at[slot, :, s], os.at[s], orr.at[s], sibling)
+        z, cols = unit(s)
+        return remote(c_hbm.at[:, z, :, cols], gathered.at[slot, :, z, :, cols], os.at[s], orr.at[s], sibling)
 
     def f_copy(d, s):
-        place = gathered.at[sources[d], :, s]
+        z, cols = unit(s)
+        place = gathered.at[sources[d], :, z, :, cols]
         return remote(place, place, fs.at[d, s], fr.at[d, s], sibling)
 
     def y_copy(s):
-        return remote(part_out.at[:, s], part_in.at[:, s], ys.at[s], yr.at[s], across)
+        z, cols = unit(s)
+        return remote(part_out.at[:, z, :, cols], part_in.at[:, z, :, cols], ys.at[s], yr.at[s], across)
 
     def l_copy(side):
         return aside(label_out.at[side], label_in.at[side], ls.at[side], lr.at[side], side)
@@ -84,12 +97,6 @@
 
     def s_copy(side, s):
         return aside(src_out.at[side, :, s], src_in.at[side, :, s], ss.at[side, s], sr.at[side, s], side)
-
-    def new_copy(s):
-        return pltpu.make_async_copy(part_in.at[:, s], new_hbm.at[:, s], new_sem.at[s])
-
-    def out_copy(s):
-        return pltpu.make_async_copy(pot.at[:, s], pot_hbm.at[:, s], out_sem.at[s])
 
     own_copy = pltpu.make_async_copy(c_hbm, gathered.at[slot], own_sem)
     label_copy = pltpu.make_async_copy(ph_hbm, labels.at[:, 0:nx], label_sem)
@@ -109,7 +116,7 @@
             x_copy(d, s).start()
         o_copy(s).start()
 
-    for s in range(min(DEPTH, nz)):
+    for s in range(min(DEPTH, units)):
         send(s)
     own_copy.wait()
     label_copy.wait()
@@ -123,9 +130,12 @@
     l_copy(0).start()
     l_copy(1).start()
 
-    def partials(s):
+    def partials(unit_index):
+        s = unit_index // PARTS
+        begin = lax.rem(unit_index, PARTS) * span
+
         def block(i, carry):
-            cols = pl.ds(pl.multiple_of(i * LANES, LANES), LANES)
+            cols = pl.ds(pl.multiple_of(begin + i * LANES, 128), LANES)
             phase = labels[s, 0:nx, cols]
             masks = [phase == p for p in range(1, phases)]
             sums = {}
@@ -147,17 +157,22 @@
                 pot[o, s, :, cols] = sums[1, o]
             return carry
 
-        lax.fori_loop(0, ny // LANES, block, 0)
-
-    def finish(s):
+        lax.fori_loop(0, span // LANES, block, 0)
+
+    def finish(unit_index):
+        s = unit_index // PARTS
+        begin = lax.rem(unit_index, PARTS) * span
+
         def block(i, carry):
-            cols = pl.ds(pl.multiple_of(i * LANES, LANES), LANES)
+            cols = pl.ds(pl.multiple_of(begin + i * LANES, 128), LANES)
             for o in range(local):
                 own = gathered[slot, o, s, :, cols]
                 pot[o, s, :, cols] = pot[o, s, :, cols] + part_in[o, s, :, cols] + own * own * own
             return carry
 
-        lax.fori_loop(0, ny // LANES, block, 0)
+        lax.fori_loop(0, span // LANES, block, 0)
+
+    def edges(s):
         for o in range(local):
             pot_out[0, o, s] = pot[o, s, nx - 1 : nx, :]
             pot_out[1, o, s] = pot[o, s, 0:1, :]
@@ -229,18 +244,63 @@
 
         lax.fori_loop(0, local, component, 0)
 
+    def planes(z):
+        @pl.when(z < nz)
+        def _():
+            edges(z)
+            for side in range(2):
+                p_copy(side, z).start()
+
+        @pl.when(z == 0)
+        def _():
+            for side in range(2):
+                l_copy(side).wait_recv()
+
+            def widen(z, carry):
+                labels[z, nx : nx + EDGE, :] = label_in[1, z]
+                labels[z, nx + EDGE : nx + 2 * EDGE, :] = label_in[0, z]
+                return carry
+
+            lax.fori_loop(0, nz, widen, 0)
+
+        w = z - 1
+
+        @pl.when((w >= 1) & (w < nz + 1))
+        def _():
+            make_source(w)
+
+        @pl.when((w - 2 >= 1) & (w - 2 < nz + 1))
+        def _():
+            take_edges(w - 2)
+
+        @pl.when((w - 3 >= 2) & (w - 3 < nz + 2))
+        def _():
+            half(source, w - 3)
+
+        @pl.when((w - 4 >= 3) & (w - 4 < nz + 3))
+        def _():
+            sweep(source, w - 4, wide, first)
+
+        @pl.when((w - 5 >= 4) & (w - 5 < nz + 4))
+        def _():
+            half(first, w - 5)
+
+        @pl.when(w - 6 >= 5)
+        def _():
+            sweep(first, w - 6, nx, fresh)
+
     def step(t, carry):
-        @pl.when(t < nz)
+        @pl.when(t < units)
         def _():
             for d in range(inner - 1):
                 x_copy(d, t).wait_recv()
                 f_copy(d, t).start()
 
-        @pl.when(t + DEPTH < nz)
+        @pl.when(t + DEPTH < units)
         def _():
             send(t + DEPTH)
 
-        @pl.when((t >= 1) & (t < nz + 1))
+        @pl.when((t >= 1) & (t < units + 1))
         def _():
             u = t - 1
             o_copy(u).wait_recv()
@@ -249,68 +309,34 @@
             partials(u)
             y_copy(u).start()
 
-        @pl.when((t >= LAG) & (t < nz + LAG))
-        def _():
-            v = t - LAG
+        v = t - LAG
+
+        @pl.when((t >= LAG) & (t < units + LAG))
+        def _():
             y_copy(v).wait_recv()
             finish(v)
-            out_copy(v).start()
-            for side in range(2):
-                p_copy(side, v).start()
-
-        @pl.when(t == LAG)
-        def _():
-            for side in range(2):
-                l_copy(side).wait_recv()
-
-            def widen(z, carry):
-                labels[z, nx : nx + EDGE, :] = label_in[1, z]
-                labels[z, nx + EDGE : nx + 2 * EDGE, :] = label_in[0, z]
-                return carry
-
-            lax.fori_loop(0, nz, widen, 0)
-
-        w = t - LAG - 2
-
-        @pl.when((w >= 1) & (w < nz + 1))
-        def _():
-            make_source(w)
-
-        @pl.when((w - 2 >= 1) & (w - 2 < nz + 1))
-        def _():
-            take_edges(w - 2)
-
-        @pl.when((w - 3 >= 2) & (w - 3 < nz + 2))
-        def _():
-            half(source, w - 3)
-
-        @pl.when((w - 4 >= 3) & (w - 4 < nz + 3))
-        def _():
-            sweep(source, w - 4, wide, first)
-
-        @pl.when((w - 5 >= 4) & (w - 5 < nz + 4))
-        def _():
-            half(first, w - 5)
-
-        @pl.when(w - 6 >= 5)
-        def _():
-            sweep(first, w - 6, nx, part_in)
-            new_copy(plane(w - 6)).start()
+
+        @pl.when((t >= LAG) & (lax.rem(t - LAG + PARTS, PARTS) == PARTS - 1))
+        def _():
+            planes(v // PARTS)
 
         return carry
 
-    lax.fori_loop(0, nz + 5 + LAG + 8, step, 0)
+    lax.fori_loop(0, LAG + units + 12 * PARTS, step, 0)
     for side in range(2):
         l_copy(side).wait_send()
 
-    def drain(s, carry):
+    def drain_units(s, carry):
         for d in range(inner - 1):
             x_copy(d, s).wait_send()
             f_copy(d, s).wait_send()
         o_copy(s).wait_send()
         y_copy(s).wait_send()
-        out_copy(s).wait()
-        new_copy(s).wait()
+        return carry
+
+    lax.fori_loop(0, units, drain_units, 0)
+
+    def drain(s, carry):
         for side in range(2):
             p_copy(side, s).wait_send()
             s_copy(side, s).wait_send()
@@ -330,18 +356,17 @@
     f32 = jnp.float32
     return pl.pallas_call(
         functools.partial(brick_kernel, inner),
-        out_shape=[jax.ShapeDtypeStruct(full, f32)] * 2,
+        out_shape=[pltpu.VMEM(full, f32)] * 2,
         in_specs=[
             pl.BlockSpec(memory_space=pl.ANY),
             pl.BlockSpec(memory_space=pl.ANY),
             pl.BlockSpec(memory_space=pltpu.SMEM),
             pl.BlockSpec(memory_space=pltpu.SMEM),
         ],
-        out_specs=[pl.BlockSpec(memory_space=pl.ANY)] * 2,
+        out_specs=[pl.BlockSpec(memory_space=pltpu.VMEM)] * 2,
         scratch_shapes=[
             pltpu.VMEM((2 * inner,) + full, f32),
             pltpu.VMEM(wide[1:], jnp.int32),
-            pltpu.VMEM(full, f32),
             pltpu.VMEM(full, f32),
             pltpu.VMEM(full, f32),
             pltpu.VMEM(wide, f32),
@@ -353,16 +378,16 @@
             pltpu.VMEM((2, local, nz, 1, ny), f32),
             pltpu.VMEM((2, local, nz, EDGE, ny), f32),
             pltpu.VMEM((2, local, nz, EDGE, ny), f32),
-            dma((inner - 1, nz)), dma((inner - 1, nz)),
-            dma((nz,)), dma((nz,)),
-            dma((inner - 1, nz)), dma((inner - 1, nz)),
-            dma((nz,)), dma((nz,)),
-            dma, dma, dma((nz,)), dma((nz,)),
+            dma((inner - 1, nz * PARTS)), dma((inner - 1, nz * PARTS)),
+            dma((nz * PARTS,)), dma((nz * PARTS,)),
+            dma((inner - 1, nz * PARTS)), dma((inner - 1, nz * PARTS)),
+            dma((nz * PARTS,)), dma((nz * PARTS,)),
+            dma, dma,
             dma((2,)), dma((2,)),
             dma((2, nz)), dma((2, nz)), dma((2, nz)), dma((2, nz)),
         ],
         compiler_params=pltpu.CompilerParams(
-            collective_id=0, has_side_effects=True, vmem_limit_bytes=60 * 2**20
+            collective_id=0, has_side_effects=True, vmem_limit_bytes=54 * 2**20
         ),
     )(concentration, phase_labels, hessian, table)
 

time: 147 us -> 140 us (0.952)
  Pallas kernels: 138 us -> 133 us
  local copies, waits for them, and re-layouts: 6.87 us -> 4.03 us
    pallas_call x1, Pallas kernels: 138 us -> 133 us  [on_device(): pl.pallas_call(functools.partial(brick_kernel, inner), out_shape=[pltpu.V...]
    unnamed x4 -> x2, local copies, waits for them, and re-layouts: 6.87 us -> 4.03 us
where the time goes in v3:
time: 140 us; the launch traced here: 139 us
  Pallas kernels  133 us (95%)
  local copies, waits for them, and re-layouts  4.03 us (3%)
    pallas_call x1, Pallas kernels, on_device(): pl.pallas_call(functools.partial(brick_kernel, inner), out_shape=[pltpu.V...  133 us
    unnamed x2, local copies, waits for them, and re-layouts  4.03 us

profile of v3, /device:TPU:0, one launch (start us, length us, event | category | flops | bytes accessed | tf_op | source)
XLA Modules:
  0.0 139.3 jit_solution(16278102596684041190)
XLA Ops:
  0.6 0.7 multiply_bitcast_fusion.1
  1.3 0.6 pad_maximum_fusion.table
  1.9 133.4 %shard_map.59 = (f32[2,16,16,2048]{3,2,1,0:T(8,128)S(1)}, f32[2,16,16,2048]{3,2,1,0:T(8,128)S(1)}) custom-call(f32[2,16,16,2048]{3,2,1,0:T(8,128)} %c_hbm.1, s32[16,16,2048]{2,1,0:T(8,128)} %ph_hbm.1, f32[4,16,16]{2,1,0:T(8,128)} %h_ref.1, f32[3,4,16]{2,1,0:T(4,128)} %pad_maximum_fusion.table), custom_call_target="tpu_custom_call" | custom-call | tf_op jit(solution)/shard_map/pallas_call | solution.py:357
  135.3 2.0 %copy.8 = f32[2,16,16,2048]{3,2,1,0:T(8,128)} copy(f32[2,16,16,2048]{3,2,1,0:T(8,128)S(1)} %get-tuple-element.5) | data formatting | bytes 8388608
  137.3 2.0 %copy.9 = f32[2,16,16,2048]{3,2,1,0:T(8,128)} copy(f32[2,16,16,2048]{3,2,1,0:T(8,128)S(1)} %get-tuple-element.6) | data formatting | bytes 8388608
